TPU v7x, 512 devices: a whole 4x4x16 slice. The times are simulated.
512 devices in a mesh: dp: 32 (over z, core), ctx: 16 (over x, y).
Axes of the slice: x: 4, y: 4, z: 16, core: 2. Of those that a mesh axis runs over, the one named last changes fastest.
Arguments:
- inputs: bfloat16 [65536, 512], P(('dp', 'ctx')), may hold values from -24 to 24
- attn_out: bfloat16 [65536, 512], P(('dp', 'ctx')), may hold values from -0.037353516 to 0.037353516
- out_grad: bfloat16 [65536, 512], P(('dp', 'ctx')), may hold values from -24 to 24
- w_uvqk: bfloat16 [512, 2048], replicated, may hold values from -0.25 to 0.25
- w_output: bfloat16 [512, 512], replicated, may hold values from -0.25 to 0.25
- norm_gain: float32 [512], replicated, may hold values from 0.1 to 1.9
- rab_table: float32 [8, 128], replicated, may hold values from -6 to 6
- bucket_map: int32 [1024], replicated, may hold values from 0 to 127, as said below
- lengths: int32 [32, 4], P('dp'), may hold values from 64 to 1024, as said below
- send_order: int32 [512, 128], P(('dp', 'ctx')), may hold values from 0 to 127, each once within a row
- recv_order: int32 [512, 128], P(('dp', 'ctx')), may hold values from 0 to 127, each once within a row
Outputs:
- grad_inputs: bfloat16 [65536, 512], P(('dp', 'ctx'))
- grad_uvqk: bfloat16 [512, 2048], P('ctx', 'dp')
- grad_output: bfloat16 [512, 512], P('ctx', 'dp')
Inputs may be any that keep to these rules, and one draw needn't show every extreme that they name: `bucket_map`: nondecreasing in the distance, 0 at distance 0, every bucket taken. `lengths`: each row sums to 2048; its longest session has exactly 1024 events. `send_order`: each row is a permutation. `recv_order`: each row is a permutation.
All inputs are finite; a program needn't handle non-finite values.
Results may differ from a plain program's by a relative error of at most 0.019.
Values may be sent and summed in bfloat16 or wider, within the bound.
A program may use at most 128 MiB of HBM per device.

v0:
```python
import jax
import jax.numpy as jnp
from jax import lax
from jax.experimental import pallas as pl
from jax.experimental.pallas import tpu as pltpu
from jax.sharding import PartitionSpec as P

MESH = pl.DeviceIdType.MESH
F32 = jnp.float32
BF16 = jnp.bfloat16

D = 512
H = 8
ROWS = 128
N_DP = 32
N_CTX = 16
N_Z = 16
TILES = 16
REACH = 8
PAIRS = 8
HALF = 8
SLOTS = 512
EARLY = 512
LATE = 768
EPS = 1e-05
LIMIT = 56 * 1024 * 1024


def mm(left, right, dims=((1,), (0,))):
    return lax.dot_general(left, right, (dims, ((), ())), preferred_element_type=F32)


def iota(shape, dim):
    return lax.broadcasted_iota(jnp.int32, shape, dim)


def slot_of(place):
    return (place >> 4) * 4 + (place & 3)


def piece_of(place):
    return (place >> 2) & 3


def sigmoid(array):
    return 1.0 / (1.0 + jnp.exp(-array))


def half_of(ctx):
    return lax.rem((ctx + 1) // 2, 2)


def member(index, half):
    return 2 * index + lax.rem(half + index, 2)


def by_piece(wide):
    piece = piece_of(iota((SLOTS, 128), 0))
    out = wide[:, :128]
    for part in range(1, 4):
        out = jnp.where(piece == part, wide[:, part * 128 : part * 128 + 128], out)
    return out


def pick_pieces(hot, flat):
    piece = piece_of(iota(hot.shape, 1))
    parts = [mm(jnp.where(piece == part, hot, 0.0).astype(BF16), flat) for part in range(4)]
    return jnp.concatenate(parts, axis=1)


def swap(array):
    return pltpu.roll(array, 64, 1)


def announce(me_dp, me_ctx):
    barrier = pltpu.get_barrier_semaphore()

    def tell_dp(step, carry):
        peer = lax.rem(me_dp + step, N_DP)
        pl.semaphore_signal(barrier, inc=1, device_id=(peer, me_ctx), device_id_type=MESH)
        return carry

    def tell_ctx(step, carry):
        peer = lax.rem(me_ctx + step, N_CTX)
        pl.semaphore_signal(barrier, inc=1, device_id=(me_dp, peer), device_id_type=MESH)
        return carry

    lax.fori_loop(1, N_DP, tell_dp, 0)
    lax.fori_loop(1, N_CTX, tell_ctx, 0)


def everyone_in():
    pl.semaphore_wait(pltpu.get_barrier_semaphore(), N_DP - 1 + N_CTX - 1)


def far_first(turn):
    return 8 + jnp.where(lax.rem(turn, 2) == 0, turn // 2, -((turn + 1) // 2))


def far_dp(me_dp, step):
    turn = step - 1
    peer_z = lax.rem(me_dp // 2 + far_first(turn // 2), N_Z)
    return 2 * peer_z + lax.rem(me_dp + 1 + turn, 2)


def spread(count, copy_to):
    def one(step, carry):
        copy_to(step).start()
        return carry

    lax.fori_loop(1, count, one, 0)


def layer_kernel(
    len_ref,
    x_hbm,
    attn_hbm,
    og_hbm,
    w_hbm,
    wo_hbm,
    gain_hbm,
    rab_hbm,
    bm_hbm,
    so_hbm,
    ro_hbm,
    rows_hbm,
    uvqk_hbm,
    output_hbm,
    x_ref,
    attn_ref,
    og_ref,
    w_ref,
    wo_ref,
    gain_ref,
    rab_ref,
    bm_ref,
    so_ref,
    ro_ref,
    sorted_rows,
    arrived,
    kv_send,
    kv_got,
    qg_send,
    qg_got,
    bias,
    turned,
    pairs,
    dqt_total,
    dkv_total,
    dkv_send,
    dkv_got,
    dqt_send,
    dqt_got,
    slope_ref,
    back_rows,
    returned,
    mixed_send,
    early_send,
    late_send,
    other_x,
    other_mixed,
    other_early,
    other_late,
    x_turned,
    mixed_turned,
    early_terms,
    early_got,
    late_terms,
    late_got,
    last_send,
    last_got,
    rows_out,
    uvqk_out,
    output_out,
    load_sem,
    send_sem,
    recv_sem,
):
    me_dp = lax.axis_index("dp")
    me_ctx = lax.axis_index("ctx")
    core = lax.rem(me_dp, 2)
    me_z = me_dp // 2
    half = half_of(me_ctx)
    own = me_ctx // 2
    partner = me_dp + 1 - 2 * core
    next_ctx = lax.rem(me_ctx + 1, N_CTX)
    next_dp = lax.rem(me_dp + 1, N_DP)

    def remote(source, target, number, dp, ctx):
        return pltpu.make_async_remote_copy(
            src_ref=source,
            dst_ref=target,
            send_sem=send_sem.at[number],
            recv_sem=recv_sem.at[number],
            device_id=(dp, ctx),
            device_id_type=MESH,
        )

    def many(source, target, number, count, dp, ctx):
        return remote(source.at[pl.ds(0, count)], target.at[pl.ds(0, count)], number, dp, ctx)

    loads = [
        pltpu.make_async_copy(source, target, load_sem.at[number])
        for number, (source, target) in enumerate(
            (
                (so_hbm, so_ref),
                (og_hbm, og_ref),
                (x_hbm, x_ref),
                (w_hbm, w_ref),
                (attn_hbm, attn_ref),
                (gain_hbm, gain_ref),
                (rab_hbm, rab_ref),
                (bm_hbm, bm_ref),
                (ro_hbm, ro_ref),
                (wo_hbm, wo_ref),
            )
        )
    ]
    for load in loads:
        load.start()
    announce(me_dp, me_ctx)
    low = iota((ROWS, 128), 1) < 64

    loads[0].wait()
    loads[1].wait()
    order = so_ref[...].astype(F32)
    lane = iota((SLOTS, 128), 1)
    place = iota((SLOTS, 128), 0)
    wanted = jnp.sum(jnp.where(lane == slot_of(place), order, 0.0), axis=1, keepdims=True)
    hot = jnp.where(lane.astype(F32) == wanted, 1.0, 0.0).astype(BF16)
    sorted_rows[...] = by_piece(mm(hot, og_ref[...])).astype(BF16).reshape(N_DP, 16, 128)
    arrived[me_dp] = sorted_rows[me_dp]
    loads[2].wait()
    everyone_in()

    def row_copy(step):
        peer = far_dp(me_dp, step)
        return remote(sorted_rows.at[peer], arrived.at[me_dp], 0, peer, me_ctx)

    spread(N_DP, row_copy)
    x_copy = remote(x_ref, other_x, 1, partner, me_ctx)
    x_copy.start()

    x = x_ref[...]
    loads[3].wait()
    pre_v = mm(x, w_ref[:, D : 2 * D])
    sig_v = sigmoid(pre_v)
    slope_ref[:, :D] = sig_v * (1.0 + pre_v * (1.0 - sig_v))
    value = pre_v * sig_v
    pre_k = mm(x, w_ref[:, 3 * D :])
    sig_k = sigmoid(pre_k)
    slope_ref[:, 2 * D :] = sig_k * (1.0 + pre_k * (1.0 - sig_k))
    key = pre_k * sig_k
    for pair in range(H // 2):
        k_two = key[:, pair * 128 : pair * 128 + 128]
        v_two = value[:, pair * 128 : pair * 128 + 128]
        kv_send[2 * pair] = jnp.where(low, k_two, swap(v_two)).astype(BF16)
        kv_send[2 * pair + 1] = jnp.where(low, swap(k_two), v_two).astype(BF16)
    kv_got[me_ctx] = kv_send[own]

    def kv_copy(step):
        peer = lax.rem(me_ctx + step, N_CTX)
        return remote(kv_send.at[peer // 2], kv_got.at[me_ctx], 2, me_dp, peer)

    spread(N_CTX, kv_copy)

    pre_u = mm(x, w_ref[:, :D])
    sig_u = sigmoid(pre_u)
    gating = (pre_u * sig_u).astype(BF16).astype(F32)
    slope_u = sig_u * (1.0 + pre_u * (1.0 - sig_u))
    pre_q = mm(x, w_ref[:, 2 * D : 3 * D])
    sig_q = sigmoid(pre_q)
    slope_ref[:, D : 2 * D] = sig_q * (1.0 + pre_q * (1.0 - sig_q))
    query = (pre_q * sig_q).astype(BF16).astype(F32) * 0.0625
    for load in loads[4:]:
        load.wait()
    gain = gain_ref[...]
    attn = attn_ref[...].astype(F32)
    centred = attn - jnp.mean(attn, axis=1, keepdims=True)
    inv_std = lax.rsqrt(jnp.mean(centred * centred, axis=1, keepdims=True) + EPS)
    normal_hat = centred * inv_std
    normed = normal_hat * gain
    mixed_send[...] = (normed * gating).astype(BF16)
    mixed_copy = remote(mixed_send, other_mixed, 3, partner, me_ctx)
    mixed_copy.start()
    gate_scale = normed * slope_u
    hat_scale = gating * gain

    buckets = iota((128, 128), 0)
    own_head = iota((H, 128), 0) == own
    lines = []
    for block in range(REACH):
        chosen = jnp.where(buckets == bm_ref[block : block + 1, :], 1.0, 0.0)
        table = lax.dot_general(
            rab_ref[...],
            chosen,
            (((1,), (0,)), ((), ())),
            precision=lax.Precision.HIGHEST,
            preferred_element_type=F32,
        )
        lines.append(jnp.sum(jnp.where(own_head, table, 0.0), axis=0, keepdims=True) * 0.5)
    blank = jnp.zeros((1, 128), F32)
    for far in range(REACH + 1):
        current = lines[far] if far < REACH else blank
        before = lines[far - 1] if far > 0 else blank
        both = jnp.broadcast_to(jnp.concatenate([current, before], axis=1), (128, 256))
        tile = pltpu.roll(both, 0, 1, stride=1, stride_axis=0)[:, :128]
        bias[(REACH + 1 - far) * 128 : (REACH + 2 - far) * 128, :] = tile
    bias[:128, :] = jnp.zeros((128, 128), F32)
    bias[(REACH + 2) * 128 :, :] = jnp.zeros((128, 128), F32)
    dqt_total[...] = jnp.zeros(dqt_total.shape, F32)

    taken = ro_ref[...].astype(F32)
    square = iota((128, 128), 0) == iota((128, 128), 1)
    slot_col = jnp.sum(jnp.where(square, taken, 0.0), axis=1, keepdims=True)
    place = iota((ROWS, SLOTS), 1)
    hot = jnp.where(slot_of(place).astype(F32) == slot_col, 1.0, 0.0)
    column = iota((D, 256), 1)
    source_row = iota((D, 256), 0)
    spread_col = (column >> 4) * 32 + (column & 15)
    pick_own = jnp.where(source_row == spread_col + 16 * core, 1.0, 0.0).astype(BF16)
    pick_else = jnp.where(source_row == spread_col + 16 * (1 - core), 1.0, 0.0).astype(BF16)
    zero_core = jnp.broadcast_to(core, (ROWS, 128)) == 0

    def by_core(first, second):
        even = jnp.where(low, first, swap(second))
        odd = jnp.where(low, swap(first), second)
        return (
            jnp.where(zero_core, even, odd).astype(BF16),
            jnp.where(zero_core, odd, even).astype(BF16),
        )

    x_turned[:, :ROWS] = x.astype(F32).T.astype(BF16)
    kv_wait = many(kv_got, kv_got, 2, N_CTX - 1, me_dp, next_ctx)
    kv_wait.wait_recv()
    for tile in range(TILES):
        flipped = kv_got[tile].astype(F32).T
        turned[:, tile * 128 : tile * 128 + 128] = flipped[:64].astype(BF16)
    x_copy.wait_recv()
    x_turned[:, ROWS:] = other_x[...].astype(F32).T.astype(BF16)
    mixed_copy.wait_recv()
    mixed_turned[:, :ROWS] = mixed_send[...].astype(F32).T.astype(BF16)
    mixed_turned[:, ROWS:] = other_mixed[...].astype(F32).T.astype(BF16)
    row_wait = many(sorted_rows, arrived, 0, N_DP - 1, next_dp, me_ctx)
    row_wait.wait_recv()
    owned = pick_pieces(hot, arrived[...].reshape(SLOTS, 128)).astype(BF16)
    grad_z = mm(owned, wo_ref[...], ((1,), (1,)))
    grad_hat = grad_z * hat_scale
    grad_attn = (
        grad_hat
        - jnp.mean(grad_hat, axis=1, keepdims=True)
        - normal_hat * jnp.mean(grad_hat * normal_hat, axis=1, keepdims=True)
    ) * inv_std
    for pair in range(H // 2):
        q_two = query[:, pair * 128 : pair * 128 + 128]
        g_two = grad_attn[:, pair * 128 : pair * 128 + 128]
        qg_send[2 * pair] = jnp.where(low, q_two, swap(g_two)).astype(BF16)
        qg_send[2 * pair + 1] = jnp.where(low, swap(q_two), g_two).astype(BF16)
    qg_got[own] = qg_send[own]

    def qg_copy(step):
        head = lax.rem(own + step, HALF)
        return remote(qg_send.at[head], qg_got.at[own], 4, me_dp, member(head, half))

    spread(HALF, qg_copy)

    gate = grad_z * gate_scale
    gate_own = []
    for block in range(2):
        first = gate[:, 256 * block : 256 * block + 128]
        second = gate[:, 256 * block + 128 : 256 * block + 256]
        kept, given = by_core(first, second)
        gate_own.append(kept)
        early_send[:, 128 * block : 128 * block + 128] = given
    early_send[:, 256:] = mm(owned, pick_else).astype(BF16)
    early_copy = remote(early_send, other_early, 5, partner, me_ctx)
    early_copy.start()
    gate_own = jnp.concatenate(gate_own, axis=1)
    owned_own = mm(owned, pick_own).astype(BF16)
    gate = gate.astype(BF16)

    early_copy.wait_recv()
    gate_both = jnp.concatenate([gate_own, other_early[:, :256]], axis=0)
    owned_both = jnp.concatenate([owned_own, other_early[:, 256:]], axis=0)
    first = mm(x_turned[...], gate_both).astype(BF16)
    early_terms[:, :, :256] = first.reshape(N_CTX, 32, 256)
    second = mm(mixed_turned[...], owned_both).astype(BF16)
    early_terms[:, :, 256:] = second.reshape(N_CTX, 32, 256)
    early_got[me_ctx] = early_terms[me_ctx]

    def early_term_copy(step):
        peer = lax.rem(me_ctx + step, N_CTX)
        return remote(early_terms.at[peer], early_got.at[me_ctx], 6, me_dp, peer)

    spread(N_CTX, early_term_copy)

    qg_wait = many(qg_send, qg_got, 4, HALF - 1, me_dp, next_ctx)
    qg_wait.wait_recv()
    for index in range(HALF):
        block = qg_got[index].astype(F32)
        pairs[index] = jnp.concatenate(
            [jnp.where(low, block, 0.0), jnp.where(low, 0.0, block)], axis=0
        ).astype(BF16)
    edge_one = len_ref[0, 0]
    edge_two = edge_one + len_ref[0, 1]
    edge_three = edge_two + len_ref[0, 2]

    dkv_total[...] = jnp.zeros(dkv_total.shape, F32)

    def meet(pair_index, index):
        keys = kv_got[pl.ds(2 * pair_index, 2)].reshape(256, 128)
        keys_turned = turned[:, pl.ds(pl.multiple_of(pair_index * 256, 256), 256)]
        tile = member(index, half)
        place = tile * 128 + iota((1, 128), 1)
        first = jnp.where(place >= edge_one, edge_one, 0)
        first = jnp.where(place >= edge_two, edge_two, first)
        first = jnp.where(place >= edge_three, edge_three, first)
        both = mm(keys, pairs[index], ((1,), (1,)))
        row = pl.multiple_of((REACH + 1 - tile + 2 * pair_index) * 128, 128)
        scores = both[:, :128] + bias[pl.ds(row, 256), :]
        bent = jnp.tanh(scores)
        key_place = pair_index * 256 + iota((256, 128), 0)
        allowed = (key_place >= first) & (key_place <= place)
        rise = jnp.where(allowed, 1.0 + bent, 0.0)
        weights = scores * rise
        slopes = (both[:, 128:] * (rise + weights * (1.0 - bent))).astype(BF16)
        dqt_total[index] += mm(keys_turned, slopes)
        found = jnp.concatenate([slopes, weights.astype(BF16)], axis=1)
        dkv_total[pair_index] += mm(found, pairs[index])

    def ship(pair_index):
        done = dkv_total[pair_index] * (1.0 / 1024.0)
        dkv_send[pl.ds(2 * pair_index, 2)] = done.astype(BF16).reshape(2, 128, 128)
        for side in range(2):
            peer = 2 * pair_index + side

            @pl.when(peer != me_ctx)
            def _():
                remote(dkv_send.at[peer], dkv_got.at[me_ctx], 7, me_dp, peer).start()

    def one_round(step, carry):
        turn = lax.rem(own + 1 + step, 6)
        for lag in range(3):
            meet(turn, turn + lag)
        meet(jnp.where(turn < 5, turn, 6), jnp.where(turn < 5, turn + 3, 6))
        meet(jnp.where(turn < 4, turn, 11 - turn), jnp.where(turn < 4, turn + 4, 7))
        ship(turn)

        @pl.when(turn >= 4)
        def _():
            ship(11 - turn)

        return carry

    lax.fori_loop(0, 6, one_round, 0)
    dkv_got[me_ctx] = dkv_send[me_ctx]
    dqt_send[...] = (dqt_total[...] * (1.0 / 16384.0)).astype(BF16)
    dqt_got[own] = dqt_send[own]

    def dqt_copy(step):
        index = lax.rem(own + step, HALF)
        return remote(dqt_send.at[index], dqt_got.at[own], 8, me_dp, member(index, half))

    spread(HALF, dqt_copy)

    slot = slot_of(iota((SLOTS, ROWS), 0))
    back_hot = jnp.where(slot == ro_ref[...], 1.0, 0.0).astype(BF16)
    sent = jnp.where(iota((ROWS, 128), 0) == so_ref[...], 1.0, 0.0).astype(BF16)
    place = iota((ROWS, SLOTS), 1)
    spot = jnp.where(iota((ROWS, SLOTS), 0) == slot_of(place), 1.0, 0.0).astype(BF16)
    final_hot = mm(sent, spot)

    dkv_wait = many(dkv_send, dkv_got, 7, N_CTX - 1, me_dp, next_ctx)
    dqt_wait = many(dqt_send, dqt_got, 8, HALF - 1, me_dp, next_ctx)
    dkv_wait.wait_recv()
    grad_k = []
    grad_v = []
    for pair in range(H // 2):
        even = dkv_got[4 * pair].astype(F32) + dkv_got[4 * pair + 1].astype(F32)
        odd = dkv_got[4 * pair + 2].astype(F32) + dkv_got[4 * pair + 3].astype(F32)
        grad_k.append(jnp.where(low, even, swap(odd)))
        grad_v.append(jnp.where(low, swap(even), odd))
    dqt_wait.wait_recv()
    grad_q = dqt_got[...].reshape(D, 128).astype(F32).T
    after = jnp.concatenate(grad_v + [grad_q] + grad_k, axis=1) * slope_ref[...]
    late_own = []
    for block in range(6):
        first = after[:, 256 * block : 256 * block + 128]
        second = after[:, 256 * block + 128 : 256 * block + 256]
        kept, given = by_core(first, second)
        late_own.append(kept)
        late_send[:, 128 * block : 128 * block + 128] = given
    late_copy = remote(late_send, other_late, 9, partner, me_ctx)
    late_copy.start()
    late_copy.wait_recv()
    late_both = jnp.concatenate([jnp.concatenate(late_own, axis=1), other_late[...]], axis=0)
    late = mm(x_turned[...], late_both).astype(BF16)
    late_terms[...] = late.reshape(N_CTX, 32, LATE)
    late_got[me_ctx] = late_terms[me_ctx]

    def late_term_copy(step):
        peer = lax.rem(me_ctx + step, N_CTX)
        return remote(late_terms.at[peer], late_got.at[me_ctx], 11, me_dp, peer)

    spread(N_CTX, late_term_copy)

    grad_pre = jnp.concatenate([gate, after.astype(BF16)], axis=1)
    branch = mm(grad_pre, w_ref[...], ((1,), (1,))).astype(BF16)
    back_rows[...] = by_piece(mm(back_hot, branch)).astype(BF16).reshape(N_DP, 16, 128)
    returned[me_dp] = back_rows[me_dp]

    def back_copy(step):
        peer = far_dp(me_dp, step)
        return remote(back_rows.at[peer], returned.at[me_dp], 10, peer, me_ctx)

    spread(N_DP, back_copy)

    early_wait = many(early_terms, early_got, 6, N_CTX - 1, me_dp, next_ctx)
    early_wait.wait_recv()
    early_sum = early_got[0].astype(F32)
    for source in range(1, N_CTX):
        early_sum = early_sum + early_got[source].astype(F32)

    back_wait = many(back_rows, returned, 10, N_DP - 1, next_dp, me_ctx)
    back_wait.wait_recv()
    arrival = pick_pieces(final_hot, returned[...].reshape(SLOTS, 128))
    rows_out[...] = (og_ref[...].astype(F32) + arrival).astype(BF16)
    rows_copy = pltpu.make_async_copy(rows_out, rows_hbm, load_sem.at[0])
    rows_copy.start()

    late_wait = many(late_terms, late_got, 11, N_CTX - 1, me_dp, next_ctx)
    late_wait.wait_recv()
    late_sum = late_got[0].astype(F32)
    for source in range(1, N_CTX):
        late_sum = late_sum + late_got[source].astype(F32)

    low = iota((32, 128), 1) < 64
    for index in range(N_Z):
        if index < 4:
            block = early_sum[:, (index // 2) * 128 : (index // 2) * 128 + 128]
        else:
            block = late_sum[:, (index // 2 - 2) * 128 : (index // 2 - 1) * 128]
        if index % 2 == 1:
            block = swap(block)
        start = 256 + (index // 8) * 128
        extra = early_sum[:, start : start + 128]
        shift = (64 - 16 * (index % 8)) % 128
        if shift:
            extra = pltpu.roll(extra, shift, 1)
        last_send[index] = jnp.where(low, block, extra).astype(BF16)
    last_got[me_z] = last_send[me_z]

    def last_copy(step):
        peer = lax.rem(me_z + far_first(step - 1), N_Z)
        return remote(last_send.at[peer], last_got.at[me_z], 12, 2 * peer + core, me_ctx)

    spread(N_Z, last_copy)
    last_wait = many(last_send, last_got, 12, N_Z - 1, 2 * lax.rem(me_z + 1, N_Z) + core, me_ctx)
    last_wait.wait_recv()
    total = last_got[0].astype(F32)
    for source in range(1, N_Z):
        total = total + last_got[source].astype(F32)
    total = total * (1.0 / 256.0)
    uvqk_out[...] = total[:, :64].astype(BF16)
    output_out[...] = total.T[64:80].astype(BF16)
    uvqk_copy = pltpu.make_async_copy(uvqk_out, uvqk_hbm, load_sem.at[1])
    output_copy = pltpu.make_async_copy(output_out, output_hbm, load_sem.at[2])
    uvqk_copy.start()
    output_copy.start()
    for copy in (
        row_wait,
        x_copy,
        kv_wait,
        mixed_copy,
        qg_wait,
        early_copy,
        early_wait,
        dkv_wait,
        dqt_wait,
        late_copy,
        back_wait,
        late_wait,
        last_wait,
    ):
        copy.wait_send()
    rows_copy.wait()
    uvqk_copy.wait()
    output_copy.wait()


def finish_kernel(rows, uvqk, output, rows_out, uvqk_out, output_out, *scratch):
    held, sems = scratch[:3], scratch[3]
    taken = [
        pltpu.make_async_copy(source, target, sems.at[number])
        for number, (source, target) in enumerate(zip((rows, uvqk, output), held))
    ]
    given = [
        pltpu.make_async_copy(source, target, sems.at[3 + number])
        for number, (source, target) in enumerate(zip(held, (rows_out, uvqk_out, output_out)))
    ]
    for copy in taken:
        copy.start()
    for first, second in zip(taken, given):
        first.wait()
        second.start()
    for copy in given:
        copy.wait()


def bf16(*shape):
    return jax.ShapeDtypeStruct(shape, BF16)


def local(
    inputs,
    attn_out,
    out_grad,
    w_uvqk,
    w_output,
    norm_gain,
    rab_table,
    bucket_map,
    lengths,
    send_order,
    recv_order,
):
    taken = (
        inputs,
        attn_out,
        out_grad,
        w_uvqk,
        w_output,
        norm_gain.reshape(1, D),
        rab_table,
        bucket_map.reshape(8, 128),
        send_order,
        recv_order,
    )
    anywhere = pl.BlockSpec(memory_space=pl.ANY)
    scratch = [pltpu.VMEM(array.shape, array.dtype) for array in taken]
    for shape, kind in (
        ((N_DP, 16, 128), BF16),
        ((N_DP, 16, 128), BF16),
        ((H, 128, 128), BF16),
        ((N_CTX, 128, 128), BF16),
        ((H, 128, 128), BF16),
        ((HALF, 128, 128), BF16),
        (((REACH + 3) * 128, 128), F32),
        ((64, TILES * 128), BF16),
        ((HALF, 256, 128), BF16),
        ((HALF, 64, 128), F32),
        ((PAIRS, 256, 128), F32),
        ((N_CTX, 128, 128), BF16),
        ((N_CTX, 128, 128), BF16),
        ((HALF, 64, 128), BF16),
        ((HALF, 64, 128), BF16),
        ((ROWS, 3 * D), F32),
        ((N_DP, 16, 128), BF16),
        ((N_DP, 16, 128), BF16),
        ((ROWS, D), BF16),
        ((ROWS, EARLY), BF16),
        ((ROWS, LATE), BF16),
        ((ROWS, D), BF16),
        ((ROWS, D), BF16),
        ((ROWS, EARLY), BF16),
        ((ROWS, LATE), BF16),
        ((D, 2 * ROWS), BF16),
        ((D, 2 * ROWS), BF16),
        ((N_CTX, 32, EARLY), BF16),
        ((N_CTX, 32, EARLY), BF16),
        ((N_CTX, 32, LATE), BF16),
        ((N_CTX, 32, LATE), BF16),
        ((N_Z, 32, 128), BF16),
        ((N_Z, 32, 128), BF16),
        ((ROWS, D), BF16),
        ((32, 64), BF16),
        ((16, 32), BF16),
    ):
        scratch.append(pltpu.VMEM(shape, kind))
    scratch += [
        pltpu.SemaphoreType.DMA((10,)),
        pltpu.SemaphoreType.DMA((13,)),
        pltpu.SemaphoreType.DMA((13,)),
    ]
    shapes = (bf16(ROWS, D), bf16(32, 64), bf16(16, 32))
    results = pl.pallas_call(
        layer_kernel,
        out_shape=shapes,
        in_specs=[pl.BlockSpec(memory_space=pltpu.SMEM)]
        + [anywhere] * len(taken),
        out_specs=(anywhere,) * 3,
        scratch_shapes=scratch,
        compiler_params=pltpu.CompilerParams(
            collective_id=0, has_side_effects=True, vmem_limit_bytes=LIMIT
        ),
    )(lengths, *taken)
    rows, uvqk, output = pl.pallas_call(
        finish_kernel,
        out_shape=shapes,
        in_specs=[anywhere] * 3,
        out_specs=(anywhere,) * 3,
        scratch_shapes=[pltpu.VMEM(shape.shape, shape.dtype) for shape in shapes]
        + [pltpu.SemaphoreType.DMA((6,))],
        compiler_params=pltpu.CompilerParams(vmem_limit_bytes=LIMIT),
    )(*results)
    return rows, uvqk, output.T


def solution(mesh):
    in_specs = (
        P(("dp", "ctx"), None),
        P(("dp", "ctx"), None),
        P(("dp", "ctx"), None),
        P(),
        P(),
        P(),
        P(),
        P(),
        P("dp", None),
        P(("dp", "ctx"), None),
        P(("dp", "ctx"), None),
    )
    out_specs = (P(("dp", "ctx"), None), P("ctx", "dp"), P("ctx", "dp"))
    return jax.shard_map(local, mesh=mesh, in_specs=in_specs, out_specs=out_specs, check_vma=False)
```

profile of v0, /device:TPU:1, one launch (start us, length us, event | category | flops | bytes accessed | tf_op | source)
XLA Modules:
  0.0 74.3 jit_solution(3731606390303836063)
XLA Ops:
  0.6 72.0 %shard_map.130 = (bf16[128,512]{1,0:T(8,128)(2,1)}, bf16[32,64]{1,0:T(8,128)(2,1)}, bf16[16,32]{1,0:T(8,128)(2,1)}) custom-call(s32[1,4]{1,0:T(1,128)} %len_ref.1, bf16[128,512]{1,0:T(8,128)(2,1)} %x_hbm.1, bf16[128,512]{1,0:T(8,128)(2,1)} %attn_hbm.1, bf16[128,512]{1,0:T(8,128)(2,1)} %og_hbm.1, bf16[512,2048]{1,0:T(8,128)(2,1)} %w_hbm.1, ...), custom_call_target="tpu_custom_call" | custom-call | tf_op jit(solution)/shard_map/pallas_call | solution.py:686
  72.7 1.6 %shard_map.131 = (bf16[128,512]{1,0:T(8,128)(2,1)}, bf16[32,64]{1,0:T(8,128)(2,1)}, bf16[16,32]{1,0:T(8,128)(2,1)}) custom-call(bf16[128,512]{1,0:T(8,128)(2,1)} %get-tuple-element.9.rows, bf16[32,64]{1,0:T(8,128)(2,1)} %get-tuple-element.10.uvqk, bf16[16,32]{1,0:T(8,128)(2,1)} %get-tuple-element.11.output), custom_call_target="tpu_custom_call" | custom-call | tf_op jit(solution)/shard_map/pallas_call | solution.py:697
where the time goes:
time: 74.4 us; the launch traced here: 74.3 us
  Pallas kernels  73.6 us (99%)
    pallas_call x1, Pallas kernels, local(): pl.pallas_call(layer_kernel, out_shape=shapes, in_specs=[pl.BlockSpec(mem...  72 us
    pallas_call x1, Pallas kernels, local(): pl.pallas_call(finish_kernel, out_shape=shapes, in_specs=[anywhere] * 3,...  1.62 us

commit v1 on v0

--- a/solution.py
+++ b/solution.py
@@ -72,11 +72,21 @@
     return pltpu.roll(array, 64, 1)
 
 
+def far_first(turn):
+    return 8 + jnp.where(lax.rem(turn, 2) == 0, turn // 2, -((turn + 1) // 2))
+
+
+def far_dp(me_dp, step):
+    turn = step - 1
+    peer_z = lax.rem(me_dp // 2 + far_first(turn // 2), N_Z)
+    return 2 * peer_z + lax.rem(me_dp + 1 + turn, 2)
+
+
 def announce(me_dp, me_ctx):
     barrier = pltpu.get_barrier_semaphore()
 
     def tell_dp(step, carry):
-        peer = lax.rem(me_dp + step, N_DP)
+        peer = far_dp(me_dp, step)
         pl.semaphore_signal(barrier, inc=1, device_id=(peer, me_ctx), device_id_type=MESH)
         return carry
 
@@ -91,16 +101,6 @@
 
 def everyone_in():
     pl.semaphore_wait(pltpu.get_barrier_semaphore(), N_DP - 1 + N_CTX - 1)
-
-
-def far_first(turn):
-    return 8 + jnp.where(lax.rem(turn, 2) == 0, turn // 2, -((turn + 1) // 2))
-
-
-def far_dp(me_dp, step):
-    turn = step - 1
-    peer_z = lax.rem(me_dp // 2 + far_first(turn // 2), N_Z)
-    return 2 * peer_z + lax.rem(me_dp + 1 + turn, 2)
 
 
 def spread(count, copy_to):
@@ -140,8 +140,10 @@
     arrived,
     kv_send,
     kv_got,
-    qg_send,
-    qg_got,
+    q_send,
+    q_got,
+    g_send,
+    g_got,
     bias,
     turned,
     pairs,
@@ -165,8 +167,16 @@
     mixed_turned,
     early_terms,
     early_got,
-    late_terms,
-    late_got,
+    early_spread,
+    early_parts,
+    late_x,
+    late_y,
+    late_gx,
+    late_gy,
+    late_mx,
+    late_my,
+    late_ex,
+    late_ey,
     last_send,
     last_got,
     rows_out,
@@ -186,6 +196,8 @@
     next_ctx = lax.rem(me_ctx + 1, N_CTX)
     next_dp = lax.rem(me_dp + 1, N_DP)
 
+    announce(me_dp, me_ctx)
+
     def remote(source, target, number, dp, ctx):
         return pltpu.make_async_remote_copy(
             src_ref=source,
@@ -195,6 +207,29 @@
             device_id=(dp, ctx),
             device_id_type=MESH,
         )
+
+    me_x = me_ctx // 4
+    me_y = lax.rem(me_ctx, 4)
+    me_w = lax.rem(me_z, 4)
+
+    def peers(step):
+        return lax.rem(me_x + step, 4), lax.rem(me_y + step, 4)
+
+    def stage_two(mid_x, mid_y, end_x, end_y, number):
+        end_x[me_y] = mid_x[me_y]
+        end_y[me_x] = mid_y[me_x]
+        for step in (2, 1, 3):
+            x, y = peers(step)
+            remote(mid_x.at[y], end_x.at[me_y], number, me_dp, 4 * me_x + y).start()
+            remote(mid_y.at[x], end_y.at[me_x], number + 1, me_dp, 4 * x + me_y).start()
+
+    def four(got):
+        return (got[0].astype(F32) + got[1].astype(F32)) + (
+            got[2].astype(F32) + got[3].astype(F32)
+        )
+
+    def fold(got, mid):
+        mid[...] = four(got).astype(BF16).reshape(4, 32, got.shape[2])
 
     def many(source, target, number, count, dp, ctx):
         return remote(source.at[pl.ds(0, count)], target.at[pl.ds(0, count)], number, dp, ctx)
@@ -218,7 +253,6 @@
     ]
     for load in loads:
         load.start()
-    announce(me_dp, me_ctx)
     low = iota((ROWS, 128), 1) < 64
 
     loads[0].wait()
@@ -272,6 +306,23 @@
     sig_q = sigmoid(pre_q)
     slope_ref[:, D : 2 * D] = sig_q * (1.0 + pre_q * (1.0 - sig_q))
     query = (pre_q * sig_q).astype(BF16).astype(F32) * 0.0625
+    top = iota((64, 128), 1) < 64
+
+    def stacked(wide, target):
+        for pair in range(H // 2):
+            upper = wide[:64, pair * 128 : pair * 128 + 128]
+            lower = wide[64:, pair * 128 : pair * 128 + 128]
+            target[2 * pair] = jnp.where(top, upper, swap(lower)).astype(BF16)
+            target[2 * pair + 1] = jnp.where(top, swap(upper), lower).astype(BF16)
+
+    stacked(query, q_send)
+    q_got[own] = q_send[own]
+
+    def q_copy(step):
+        head = lax.rem(own + step, HALF)
+        return remote(q_send.at[head], q_got.at[own], 9, me_dp, member(head, half))
+
+    spread(HALF, q_copy)
     for load in loads[4:]:
         load.wait()
     gain = gain_ref[...]
@@ -309,6 +360,7 @@
     bias[:128, :] = jnp.zeros((128, 128), F32)
     bias[(REACH + 2) * 128 :, :] = jnp.zeros((128, 128), F32)
     dqt_total[...] = jnp.zeros(dqt_total.shape, F32)
+    dkv_total[...] = jnp.zeros(dkv_total.shape, F32)
 
     taken = ro_ref[...].astype(F32)
     square = iota((128, 128), 0) == iota((128, 128), 1)
@@ -331,11 +383,6 @@
         )
 
     x_turned[:, :ROWS] = x.astype(F32).T.astype(BF16)
-    kv_wait = many(kv_got, kv_got, 2, N_CTX - 1, me_dp, next_ctx)
-    kv_wait.wait_recv()
-    for tile in range(TILES):
-        flipped = kv_got[tile].astype(F32).T
-        turned[:, tile * 128 : tile * 128 + 128] = flipped[:64].astype(BF16)
     x_copy.wait_recv()
     x_turned[:, ROWS:] = other_x[...].astype(F32).T.astype(BF16)
     mixed_copy.wait_recv()
@@ -351,18 +398,14 @@
         - jnp.mean(grad_hat, axis=1, keepdims=True)
         - normal_hat * jnp.mean(grad_hat * normal_hat, axis=1, keepdims=True)
     ) * inv_std
-    for pair in range(H // 2):
-        q_two = query[:, pair * 128 : pair * 128 + 128]
-        g_two = grad_attn[:, pair * 128 : pair * 128 + 128]
-        qg_send[2 * pair] = jnp.where(low, q_two, swap(g_two)).astype(BF16)
-        qg_send[2 * pair + 1] = jnp.where(low, swap(q_two), g_two).astype(BF16)
-    qg_got[own] = qg_send[own]
-
-    def qg_copy(step):
+    stacked(grad_attn, g_send)
+    g_got[own] = g_send[own]
+
+    def g_copy(step):
         head = lax.rem(own + step, HALF)
-        return remote(qg_send.at[head], qg_got.at[own], 4, me_dp, member(head, half))
-
-    spread(HALF, qg_copy)
+        return remote(g_send.at[head], g_got.at[own], 4, me_dp, member(head, half))
+
+    spread(HALF, g_copy)
 
     gate = grad_z * gate_scale
     gate_own = []
@@ -379,33 +422,48 @@
     owned_own = mm(owned, pick_own).astype(BF16)
     gate = gate.astype(BF16)
 
+    kv_wait = many(kv_got, kv_got, 2, N_CTX - 1, me_dp, next_ctx)
+    kv_wait.wait_recv()
+    for tile in range(TILES):
+        flipped = kv_got[tile].astype(F32).T
+        turned[:, tile * 128 : tile * 128 + 128] = flipped[:64].astype(BF16)
     early_copy.wait_recv()
     gate_both = jnp.concatenate([gate_own, other_early[:, :256]], axis=0)
     owned_both = jnp.concatenate([owned_own, other_early[:, 256:]], axis=0)
-    first = mm(x_turned[...], gate_both).astype(BF16)
-    early_terms[:, :, :256] = first.reshape(N_CTX, 32, 256)
-    second = mm(mixed_turned[...], owned_both).astype(BF16)
-    early_terms[:, :, 256:] = second.reshape(N_CTX, 32, 256)
-    early_got[me_ctx] = early_terms[me_ctx]
-
-    def early_term_copy(step):
-        peer = lax.rem(me_ctx + step, N_CTX)
-        return remote(early_terms.at[peer], early_got.at[me_ctx], 6, me_dp, peer)
-
-    spread(N_CTX, early_term_copy)
-
-    qg_wait = many(qg_send, qg_got, 4, HALF - 1, me_dp, next_ctx)
-    qg_wait.wait_recv()
+    first = mm(x_turned[...], gate_both)
+    second = mm(mixed_turned[...], owned_both)
+    left = iota((D, 128), 1) < 64
+    for pair in range(2):
+        gate_two = first[:, 128 * pair : 128 * pair + 128]
+        out_two = second[:, 128 * pair : 128 * pair + 128]
+        early_terms[2 * pair] = jnp.where(left, gate_two, swap(out_two)).astype(BF16)
+        early_terms[2 * pair + 1] = jnp.where(left, swap(gate_two), out_two).astype(BF16)
+    early_got[me_w] = early_terms[me_w]
+    for step in (2, 1, 3):
+        peer = lax.rem(me_w + step, 4)
+        remote(
+            early_terms.at[peer],
+            early_got.at[me_w],
+            6,
+            2 * (me_z - me_w + peer) + core,
+            me_ctx,
+        ).start()
+
+    q_wait = many(q_send, q_got, 9, HALF - 1, me_dp, next_ctx)
+    g_wait = many(g_send, g_got, 4, HALF - 1, me_dp, next_ctx)
+    q_wait.wait_recv()
     for index in range(HALF):
-        block = qg_got[index].astype(F32)
-        pairs[index] = jnp.concatenate(
-            [jnp.where(low, block, 0.0), jnp.where(low, 0.0, block)], axis=0
-        ).astype(BF16)
+        block = q_got[index].astype(F32)
+        pairs[index, :64] = jnp.where(top, block, 0.0).astype(BF16)
+        pairs[index, 64:128] = jnp.where(top, swap(block), 0.0).astype(BF16)
+    g_wait.wait_recv()
+    for index in range(HALF):
+        block = g_got[index].astype(F32)
+        pairs[index, 128:192] = jnp.where(top, 0.0, swap(block)).astype(BF16)
+        pairs[index, 192:] = jnp.where(top, 0.0, block).astype(BF16)
     edge_one = len_ref[0, 0]
     edge_two = edge_one + len_ref[0, 1]
     edge_three = edge_two + len_ref[0, 2]
-
-    dkv_total[...] = jnp.zeros(dkv_total.shape, F32)
 
     def meet(pair_index, index):
         keys = kv_got[pl.ds(2 * pair_index, 2)].reshape(256, 128)
@@ -436,7 +494,7 @@
 
             @pl.when(peer != me_ctx)
             def _():
-                remote(dkv_send.at[peer], dkv_got.at[me_ctx], 7, me_dp, peer).start()
+                remote(dkv_send.at[peer], dkv_got.at[me_ctx], 14, me_dp, peer).start()
 
     def one_round(step, carry):
         turn = lax.rem(own + 1 + step, 6)
@@ -459,7 +517,7 @@
 
     def dqt_copy(step):
         index = lax.rem(own + step, HALF)
-        return remote(dqt_send.at[index], dqt_got.at[own], 8, me_dp, member(index, half))
+        return remote(dqt_send.at[index], dqt_got.at[own], 15, me_dp, member(index, half))
 
     spread(HALF, dqt_copy)
 
@@ -470,8 +528,8 @@
     spot = jnp.where(iota((ROWS, SLOTS), 0) == slot_of(place), 1.0, 0.0).astype(BF16)
     final_hot = mm(sent, spot)
 
-    dkv_wait = many(dkv_send, dkv_got, 7, N_CTX - 1, me_dp, next_ctx)
-    dqt_wait = many(dqt_send, dqt_got, 8, HALF - 1, me_dp, next_ctx)
+    dkv_wait = many(dkv_send, dkv_got, 14, N_CTX - 1, me_dp, next_ctx)
+    dqt_wait = many(dqt_send, dqt_got, 15, HALF - 1, me_dp, next_ctx)
     dkv_wait.wait_recv()
     grad_k = []
     grad_v = []
@@ -480,30 +538,57 @@
         odd = dkv_got[4 * pair + 2].astype(F32) + dkv_got[4 * pair + 3].astype(F32)
         grad_k.append(jnp.where(low, even, swap(odd)))
         grad_v.append(jnp.where(low, swap(even), odd))
+    after_v = jnp.concatenate(grad_v, axis=1) * slope_ref[:, :D]
+    after_k = jnp.concatenate(grad_k, axis=1) * slope_ref[:, 2 * D :]
+    late_own = []
+
+    def split_late(wide, start):
+        for block in range(2):
+            kept, given = by_core(
+                wide[:, 256 * block : 256 * block + 128],
+                wide[:, 256 * block + 128 : 256 * block + 256],
+            )
+            late_own.append(kept)
+            late_send[:, start + 128 * block : start + 128 * block + 128] = given
+
+    split_late(after_v, 0)
+    split_late(after_k, 256)
+    late_copy = remote(
+        late_send.at[:, pl.ds(0, 512)], other_late.at[:, pl.ds(0, 512)], 16, partner, me_ctx
+    )
+    late_copy.start()
     dqt_wait.wait_recv()
-    grad_q = dqt_got[...].reshape(D, 128).astype(F32).T
-    after = jnp.concatenate(grad_v + [grad_q] + grad_k, axis=1) * slope_ref[...]
-    late_own = []
-    for block in range(6):
-        first = after[:, 256 * block : 256 * block + 128]
-        second = after[:, 256 * block + 128 : 256 * block + 256]
-        kept, given = by_core(first, second)
-        late_own.append(kept)
-        late_send[:, 128 * block : 128 * block + 128] = given
-    late_copy = remote(late_send, other_late, 9, partner, me_ctx)
-    late_copy.start()
+    after_q = dqt_got[...].reshape(D, 128).astype(F32).T * slope_ref[:, D : 2 * D]
+    split_late(after_q, 512)
+    query_copy = remote(
+        late_send.at[:, pl.ds(512, 256)], other_late.at[:, pl.ds(512, 256)], 8, partner, me_ctx
+    )
+    query_copy.start()
     late_copy.wait_recv()
-    late_both = jnp.concatenate([jnp.concatenate(late_own, axis=1), other_late[...]], axis=0)
+    late_both = jnp.concatenate(
+        [jnp.concatenate(late_own[:4], axis=1), other_late[:, :512]], axis=0
+    )
     late = mm(x_turned[...], late_both).astype(BF16)
-    late_terms[...] = late.reshape(N_CTX, 32, LATE)
-    late_got[me_ctx] = late_terms[me_ctx]
-
-    def late_term_copy(step):
-        peer = lax.rem(me_ctx + step, N_CTX)
-        return remote(late_terms.at[peer], late_got.at[me_ctx], 11, me_dp, peer)
-
-    spread(N_CTX, late_term_copy)
-
+    late_x[...] = late[:, :384].reshape(4, 128, 384)
+    late_gx[me_x] = late_x[me_x]
+    for step in (2, 1, 3):
+        x, y = peers(step)
+        remote(late_x.at[x], late_gx.at[me_x], 10, me_dp, 4 * x + me_y).start()
+    query_copy.wait_recv()
+    query_both = jnp.concatenate(
+        [jnp.concatenate(late_own[4:], axis=1), other_late[:, 512:]], axis=0
+    )
+    late_q = mm(x_turned[...], query_both).astype(BF16)
+    for x in range(4):
+        for y in range(4):
+            row = (4 * x + y) * 32
+            late_y[y, 32 * x : 32 * x + 32, :128] = late[row : row + 32, 384:]
+            late_y[y, 32 * x : 32 * x + 32, 128:] = late_q[row : row + 32, :]
+    late_gy[me_y] = late_y[me_y]
+    for step in (2, 1, 3):
+        x, y = peers(step)
+        remote(late_y.at[y], late_gy.at[me_y], 11, me_dp, 4 * me_x + y).start()
+    after = jnp.concatenate([after_v, after_q, after_k], axis=1)
     grad_pre = jnp.concatenate([gate, after.astype(BF16)], axis=1)
     branch = mm(grad_pre, w_ref[...], ((1,), (1,))).astype(BF16)
     back_rows[...] = by_piece(mm(back_hot, branch)).astype(BF16).reshape(N_DP, 16, 128)
@@ -511,51 +596,73 @@
 
     def back_copy(step):
         peer = far_dp(me_dp, step)
-        return remote(back_rows.at[peer], returned.at[me_dp], 10, peer, me_ctx)
+        return remote(back_rows.at[peer], returned.at[me_dp], 17, peer, me_ctx)
 
     spread(N_DP, back_copy)
 
-    early_wait = many(early_terms, early_got, 6, N_CTX - 1, me_dp, next_ctx)
+    early_wait = many(early_terms, early_got, 6, 3, partner, me_ctx)
     early_wait.wait_recv()
-    early_sum = early_got[0].astype(F32)
-    for source in range(1, N_CTX):
-        early_sum = early_sum + early_got[source].astype(F32)
-
-    back_wait = many(back_rows, returned, 10, N_DP - 1, next_dp, me_ctx)
+    early_spread[...] = four(early_got).astype(BF16).reshape(N_CTX, 32, 128)
+    early_parts[me_ctx] = early_spread[me_ctx]
+
+    def early_part_copy(step):
+        peer = lax.rem(me_ctx + step, N_CTX)
+        return remote(early_spread.at[peer], early_parts.at[me_ctx], 7, me_dp, peer)
+
+    spread(N_CTX, early_part_copy)
+
+    late_wait = [
+        many(late_x, late_gx, 10, 3, me_dp, next_ctx),
+        many(late_y, late_gy, 11, 3, me_dp, next_ctx),
+    ]
+    for copy in late_wait:
+        copy.wait_recv()
+    fold(late_gx, late_mx)
+    fold(late_gy, late_my)
+    stage_two(late_mx, late_my, late_ex, late_ey, 12)
+    back_wait = many(back_rows, returned, 17, N_DP - 1, next_dp, me_ctx)
     back_wait.wait_recv()
     arrival = pick_pieces(final_hot, returned[...].reshape(SLOTS, 128))
     rows_out[...] = (og_ref[...].astype(F32) + arrival).astype(BF16)
     rows_copy = pltpu.make_async_copy(rows_out, rows_hbm, load_sem.at[0])
     rows_copy.start()
 
-    late_wait = many(late_terms, late_got, 11, N_CTX - 1, me_dp, next_ctx)
-    late_wait.wait_recv()
-    late_sum = late_got[0].astype(F32)
+    early_end = many(early_spread, early_parts, 7, N_CTX - 1, me_dp, next_ctx)
+    early_end.wait_recv()
+    early_sum = early_parts[0].astype(F32)
     for source in range(1, N_CTX):
-        late_sum = late_sum + late_got[source].astype(F32)
+        early_sum = early_sum + early_parts[source].astype(F32)
+    late_end = [
+        many(late_mx, late_ex, 12, 3, me_dp, next_ctx),
+        many(late_my, late_ey, 13, 3, me_dp, next_ctx),
+    ]
+    for copy in late_end:
+        copy.wait_recv()
+    late_sum = jnp.concatenate([four(late_ex), four(late_ey)], axis=1)
 
     low = iota((32, 128), 1) < 64
+    group = jnp.broadcast_to(me_w, (32, 128))
     for index in range(N_Z):
         if index < 4:
-            block = early_sum[:, (index // 2) * 128 : (index // 2) * 128 + 128]
+            block = jnp.where(group == index, early_sum, 0.0)
         else:
-            block = late_sum[:, (index // 2 - 2) * 128 : (index // 2 - 1) * 128]
-        if index % 2 == 1:
-            block = swap(block)
-        start = 256 + (index // 8) * 128
-        extra = early_sum[:, start : start + 128]
-        shift = (64 - 16 * (index % 8)) % 128
-        if shift:
-            extra = pltpu.roll(extra, shift, 1)
+            spot = index - 4 if index < 8 else (index if index < 12 else index - 8)
+            block = late_sum[:, (spot // 2) * 128 : (spot // 2) * 128 + 128]
+            if spot % 2 == 1:
+                block = swap(block)
+        extra = early_sum
+        if index % 4:
+            extra = pltpu.roll(extra, 128 - 16 * (index % 4), 1)
+        extra = jnp.where(group == index // 4, extra, 0.0)
         last_send[index] = jnp.where(low, block, extra).astype(BF16)
     last_got[me_z] = last_send[me_z]
 
     def last_copy(step):
         peer = lax.rem(me_z + far_first(step - 1), N_Z)
-        return remote(last_send.at[peer], last_got.at[me_z], 12, 2 * peer + core, me_ctx)
+        return remote(last_send.at[peer], last_got.at[me_z], 18, 2 * peer + core, me_ctx)
 
     spread(N_Z, last_copy)
-    last_wait = many(last_send, last_got, 12, N_Z - 1, 2 * lax.rem(me_z + 1, N_Z) + core, me_ctx)
+    last_wait = many(last_send, last_got, 18, N_Z - 1, 2 * lax.rem(me_z + 1, N_Z) + core, me_ctx)
     last_wait.wait_recv()
     total = last_got[0].astype(F32)
     for source in range(1, N_Z):
@@ -572,15 +679,19 @@
         x_copy,
         kv_wait,
         mixed_copy,
-        qg_wait,
+        q_wait,
+        g_wait,
         early_copy,
-        early_wait,
         dkv_wait,
         dqt_wait,
         late_copy,
+        query_copy,
+        early_wait,
+        early_end,
         back_wait,
-        late_wait,
         last_wait,
+        *late_wait,
+        *late_end,
     ):
         copy.wait_send()
     rows_copy.wait()
@@ -643,8 +754,7 @@
         ((N_DP, 16, 128), BF16),
         ((H, 128, 128), BF16),
         ((N_CTX, 128, 128), BF16),
-        ((H, 128, 128), BF16),
-        ((HALF, 128, 128), BF16),
+        *(((HALF, 64, 128), BF16),) * 4,
         (((REACH + 3) * 128, 128), F32),
         ((64, TILES * 128), BF16),
         ((HALF, 256, 128), BF16),
@@ -666,10 +776,12 @@
         ((ROWS, LATE), BF16),
         ((D, 2 * ROWS), BF16),
         ((D, 2 * ROWS), BF16),
-        ((N_CTX, 32, EARLY), BF16),
-        ((N_CTX, 32, EARLY), BF16),
-        ((N_CTX, 32, LATE), BF16),
-        ((N_CTX, 32, LATE), BF16),
+        ((4, D, 128), BF16),
+        ((4, D, 128), BF16),
+        ((N_CTX, 32, 128), BF16),
+        ((N_CTX, 32, 128), BF16),
+        *(((4, 128, LATE // 2), BF16),) * 4,
+        *(((4, 32, LATE // 2), BF16),) * 4,
         ((N_Z, 32, 128), BF16),
         ((N_Z, 32, 128), BF16),
         ((ROWS, D), BF16),
@@ -679,8 +791,8 @@
         scratch.append(pltpu.VMEM(shape, kind))
     scratch += [
         pltpu.SemaphoreType.DMA((10,)),
-        pltpu.SemaphoreType.DMA((13,)),
-        pltpu.SemaphoreType.DMA((13,)),
+        pltpu.SemaphoreType.DMA((19,)),
+        pltpu.SemaphoreType.DMA((19,)),
     ]
     shapes = (bf16(ROWS, D), bf16(32, 64), bf16(16, 32))
     results = pl.pallas_call(

time: 74.4 us -> 68.3 us (0.918); the launches traced: 74.3 us -> 67.4 us
  Pallas kernels: 73.6 us -> 66.7 us
    pallas_call x1, Pallas kernels: 72 us -> 65.1 us  [local(): pl.pallas_call(layer_kernel, out_shape=shapes, in_specs=[pl.BlockSpec(mem...]
where the time goes in v1:
time: 68.3 us; the launch traced here: 67.4 us
  Pallas kernels  66.7 us (98%)
    pallas_call x1, Pallas kernels, local(): pl.pallas_call(layer_kernel, out_shape=shapes, in_specs=[pl.BlockSpec(mem...  65.1 us
    pallas_call x1, Pallas kernels, local(): pl.pallas_call(finish_kernel, out_shape=shapes, in_specs=[anywhere] * 3,...  1.62 us

profile of v1, /device:TPU:1, one launch (start us, length us, event | category | flops | bytes accessed | tf_op | source)
XLA Modules:
  0.0 67.4 jit_solution(14491704008622823742)
XLA Ops:
  0.6 65.1 %shard_map.130 = (bf16[128,512]{1,0:T(8,128)(2,1)}, bf16[32,64]{1,0:T(8,128)(2,1)}, bf16[16,32]{1,0:T(8,128)(2,1)}) custom-call(s32[1,4]{1,0:T(1,128)} %len_ref.1, bf16[128,512]{1,0:T(8,128)(2,1)} %x_hbm.1, bf16[128,512]{1,0:T(8,128)(2,1)} %attn_hbm.1, bf16[128,512]{1,0:T(8,128)(2,1)} %og_hbm.1, bf16[512,2048]{1,0:T(8,128)(2,1)} %w_hbm.1, ...), custom_call_target="tpu_custom_call" | custom-call | tf_op jit(solution)/shard_map/pallas_call | solution.py:798
  65.8 1.6 %shard_map.131 = (bf16[128,512]{1,0:T(8,128)(2,1)}, bf16[32,64]{1,0:T(8,128)(2,1)}, bf16[16,32]{1,0:T(8,128)(2,1)}) custom-call(bf16[128,512]{1,0:T(8,128)(2,1)} %get-tuple-element.9.rows, bf16[32,64]{1,0:T(8,128)(2,1)} %get-tuple-element.10.uvqk, bf16[16,32]{1,0:T(8,128)(2,1)} %get-tuple-element.11.output), custom_call_target="tpu_custom_call" | custom-call | tf_op jit(solution)/shard_map/pallas_call | solution.py:809
